TPU v7x, 256 devices: a whole 4x4x8 slice. The times are simulated.
256 devices in a mesh: ctx: 32 (over z, x), tp: 8 (over y, core).
Axes of the slice: x: 4, y: 4, z: 8, core: 2. Of those that a mesh axis runs over, the one named last changes fastest.
Arguments:
- query_in: bfloat16 [16384, 8192], P('ctx', 'tp'), may hold values from -6 to 6
- key_in: bfloat16 [16384, 8192], P('ctx', 'tp'), may hold values from -6 to 6
- value_in: bfloat16 [16384, 8192], P('ctx', 'tp'), may hold values from -6 to 6
- filters: bfloat16 [512, 128], P('tp'), may hold values from -0.5 to 0.5
- proj_out: bfloat16 [4096, 8192], P('ctx', 'tp'), may hold values from -0.0625 to 0.0625
- cotangent: bfloat16 [16384, 4096], P('ctx', 'tp'), may hold values from -6 to 6
Outputs:
- grad_query: bfloat16 [16384, 8192], P('ctx', 'tp')
- grad_key: bfloat16 [16384, 8192], P('ctx', 'tp')
- grad_value: bfloat16 [16384, 8192], P('ctx', 'tp')
- grad_filter: float32 [512, 128], P('tp')
- grad_proj: float32 [4096, 8192], P('ctx', 'tp')
All inputs are finite; a program needn't handle non-finite values.
Results may differ from a plain program's by a relative error of at most 0.005.
Values may be sent and summed in bfloat16 or wider, within the bound.
No kernel may reach another device: no remote copies, remote signals or barrier semaphores. Data moves between devices by JAX's collectives and lax.ppermute only.
A program may use at most 192 MiB of HBM per device.

v0:
```python
import jax
import jax.numpy as jnp
from jax import lax
from jax.sharding import PartitionSpec as P


def from_behind(value, axis, by):
    count = lax.axis_size(axis)
    pairs = [(i, i + by) for i in range(count) if 0 <= i + by < count]
    return lax.ppermute(value, axis, pairs)


def toeplitz_rows(filters):
    group_count, tap_count = filters.shape
    padded = jnp.concatenate(
        [
            jnp.zeros((group_count, 1), filters.dtype),
            jnp.flip(filters, 1),
            jnp.zeros((group_count, 2 * tap_count - 1), filters.dtype),
        ],
        1,
    )
    tiled = jnp.tile(padded, (1, tap_count))[:, : tap_count * (3 * tap_count - 1)]
    return tiled.reshape(group_count, tap_count, 3 * tap_count - 1)[:, :, : 2 * tap_count]


def on_device(query_in, key_in, value_in, filters, proj_out, cotangent):
    tok_rows, chan_width = query_in.shape
    group_count, tap_count = filters.shape
    group_size = chan_width // group_count
    blocks = tok_rows // tap_count
    table = toeplitz_rows(filters)
    mixed_in = (key_in.astype(jnp.float32) * value_in.astype(jnp.float32)).astype(jnp.bfloat16)
    left_rim = from_behind(mixed_in[tok_rows - tap_count + 1 :], "ctx", 1)
    extended = jnp.concatenate(
        [jnp.zeros((1, chan_width), jnp.bfloat16), left_rim, mixed_in[: tok_rows - tap_count]], 0
    )
    window = jnp.concatenate(
        [
            extended.reshape(blocks, tap_count, group_count, group_size),
            mixed_in.reshape(blocks, tap_count, group_count, group_size),
        ],
        1,
    )
    conv_out = jnp.einsum(
        "gts,bsgc->btgc", table, window, preferred_element_type=jnp.float32
    ).reshape(tok_rows, chan_width)
    gated = (query_in.astype(jnp.float32) * conv_out).astype(jnp.bfloat16)
    cot_full = lax.all_gather(cotangent, "tp", axis=1, tiled=True)
    columns = cot_full
    grad_all = jnp.dot(
        columns,
        lax.all_gather(proj_out, "ctx", axis=0, tiled=True),
        preferred_element_type=jnp.float32,
    )
    grad_query = (grad_all * conv_out).astype(jnp.bfloat16)
    grad_inner = (grad_all * query_in.astype(jnp.float32)).astype(jnp.bfloat16)
    next_rows = from_behind(grad_inner[: tap_count - 1], "ctx", -1)
    ahead = jnp.concatenate(
        [grad_inner[tap_count:], next_rows, jnp.zeros((1, chan_width), jnp.bfloat16)], 0
    )
    inner_blocks = grad_inner.reshape(blocks, tap_count, group_count, group_size)
    ahead_blocks = ahead.reshape(blocks, tap_count, group_count, group_size)
    grad_mixed = jnp.einsum(
        "gts,btgc->bsgc", table[:, :, tap_count:], inner_blocks, preferred_element_type=jnp.float32
    )
    grad_mixed = grad_mixed + jnp.einsum(
        "gts,btgc->bsgc", table[:, :, :tap_count], ahead_blocks, preferred_element_type=jnp.float32
    )
    grad_mixed = grad_mixed.reshape(tok_rows, chan_width)
    grad_key = (grad_mixed * value_in.astype(jnp.float32)).astype(jnp.bfloat16)
    grad_value = (grad_mixed * key_in.astype(jnp.float32)).astype(jnp.bfloat16)
    corr = jnp.einsum("btgc,bsgc->gts", inner_blocks, window, preferred_element_type=jnp.float32)
    skewed = jnp.pad(corr.reshape(group_count, -1), ((0, 0), (0, tap_count))).reshape(
        group_count, tap_count, 2 * tap_count + 1
    )
    filter_part = jnp.flip(jnp.sum(skewed, axis=1)[:, 1 : tap_count + 1], 1)
    columns = cot_full
    grad_proj = lax.psum_scatter(
        lax.dot_general(
            columns, gated, (((0,), (0,)), ((), ())), preferred_element_type=jnp.float32
        ),
        "ctx",
        scatter_dimension=0,
        tiled=True,
    )
    grad_filter = lax.psum(filter_part, "ctx")
    return (grad_query, grad_key, grad_value, grad_filter, grad_proj)


def solution(mesh):
    placed = (
        P("ctx", "tp"),
        P("ctx", "tp"),
        P("ctx", "tp"),
        P("tp", None),
        P("ctx", "tp"),
        P("ctx", "tp"),
    )
    return jax.shard_map(
        on_device,
        mesh=mesh,
        in_specs=placed,
        out_specs=(P("ctx", "tp"), P("ctx", "tp"), P("ctx", "tp"), P("tp", None), P("ctx", "tp")),
        check_vma=False,
    )
```

profile of v0, /device:TPU:8, one launch (start us, length us, event | category | flops | bytes accessed | tf_op | source)
XLA Modules:
  0.0 496.2 jit_solution(13362791816464786184)
XLA Ops:
  8.7 37.7 %all-gather.3.cloned.1.call-done = bf16[512,4096]{1,0:T(8,128)(2,1)} async-done(((bf16[512,512]{1,0:T(8,128)(2,1)}), bf16[512,4096]{1,0:T(8,128)(2,1)}) %all-gather.3.cloned.1.call-update) | async-done | bytes 4194320 | tf_op jit(solution)/shard_map/all_gather | solution.py:49
  46.4 101.9 %all-gather.5.cloned.1.call-done = bf16[4096,1024]{1,0:T(8,128)(2,1)} async-done(((bf16[128,1024]{1,0:T(8,128)(2,1)}), bf16[4096,1024]{1,0:T(8,128)(2,1)}) %all-gather.5.cloned.1.call-update) | async-done | bytes 8388624 | tf_op jit(solution)/shard_map/all_gather | solution.py:53
  148.3 10.6 %fusion.4 = (bf16[512,1024]{1,0:T(8,128)(2,1)S(1)}, f32[512,1024]{1,0:T(8,128)}) fusion(bf16[512,1024]{1,0:T(8,128)(2,1)} %param.6, bf16[512,4096]{1,0:T(8,128)(2,1)} %all-gather.3.cloned.1.call-done, bf16[4096,1024]{1,0:T(8,128)(2,1)} %all-gather.5.cloned.1.call-done), kind=kOutput, calls=%fused_computation.11 | convolution fusion | flops 4296540160 | bytes 16777216 | tf_op jit(solution)/shard_map/dot_general | solution.py:51
  161.2 2.3 copy.17
  164.2 4.1 copy.37
  168.2 3.1 slice.40
  171.3 16.4 %reshape.43 = bf16[64,128,383]{2,1,0:T(8,128)(2,1)} reshape(bf16[64,49024]{1,0:T(8,128)(2,1)} %slice.40) | data formatting | bytes 12550144 | tf_op jit(solution)/shard_map/reshape | solution.py:24
  195.5 2.3 fusion.6
  197.7 2.3 add_bitcast_fusion
  203.4 5.3 %collective-permute-start = (bf16[127,1024]{0,1:T(8,128)(2,1)S(1)}, bf16[127,1024]{0,1:T(8,128)(2,1)}, u32[]{:S(2)}, u32[]{:S(2)}) collective-permute-start(bf16[127,1024]{0,1:T(8,128)(2,1)S(1)} %slice.38), channel_id=1, source_target_pairs={{0,8},{8,16},{16,24},{24,32},{32,40},{40,48},{48,56},{56,64},{64,7... | collective-permute-start | bytes 780296 | tf_op jit(solution)/shard_map/ppermute | solution.py:10
  209.9 2.9 collective-permute-done
  212.8 2.5 pad_maximum_fusion
  217.3 4.5 fusion.8
  226.3 12.8 %convolution_bitcast_fusion = f32[4096,1024]{0,1:T(8,128)} fusion(bf16[512,4096]{1,0:T(8,128)(2,1)} %all-gather.3.cloned.1.call-done, f32[512,1024]{1,0:T(8,128)S(1)} %copy.22, bf16[512,1024]{1,0:T(8,128)(2,1)} %param.6), kind=kOutput, calls=%fused_computation | convolution fusion | flops 4296540160 | bytes 24117248 | tf_op jit(solution)/shard_map/dot_general | solution.py:80
  239.1 2.3 copy.31
  241.4 2.3 copy.30
  243.7 2.9 fusion.11
  246.6 4.7 copy.40
  251.3 3.9 pad.4
  255.2 14.2 %reshape.49 = f32[64,128,257]{2,1,0:T(8,128)} reshape(f32[64,32896]{1,0:T(8,128)} %pad.4) | data formatting | bytes 16842752 | tf_op jit(solution)/shard_map/reshape | solution.py:74
  269.4 6.2 %reduce_sum.9 = f32[64,257]{1,0:T(8,128)S(1)} reduce(f32[64,128,257]{2,1,0:T(8,128)} %reshape.49, f32[]{:T(128)} %constant.3.clone.1), dimensions={1}, to_apply=%region_0.1 | reduce | flops 2088896 | bytes 8487172 | tf_op jit(solution)/shard_map/reduce_sum | solution.py:77
  275.8 143.0 %psum.7 = f32[64,128]{1,0:T(8,128)} all-reduce(f32[64,128]{1,0:T(8,128)S(1)} %rev.9), channel_id=1, replica_groups=mesh['ctx'=32,'tp'=8] {'ctx'}, use_global_device_ids=true, to_apply=%region_1.2 | all-reduce | flops 8192 | bytes 65536 | tf_op jit(solution)/shard_map/psum | solution.py:87
  418.7 2.9 multiply_convert_fusion
  421.6 66.0 %reduce-scatter.2.cloned.1.call-done = f32[128,1024]{0,1:T(8,128)} async-done(((f32[4096,1024]{0,1:T(8,128)}), f32[128,1024]{0,1:T(8,128)}) %reduce-scatter.2.cloned.1.call-update) | async-done | bytes 524304 | tf_op jit(solution)/shard_map/reduce_scatter | solution.py:79
  (46 shorter events, 25.3 us)
Async XLA Ops:
  7.2 39.2 %all-gather.3.cloned.1.call-start = ((), (), s32[]{:S(2)}) async-start(), calls=%async_computation.1 | async-start | bytes 4718592 | tf_op jit(solution)/shard_map/all_gather | solution.py:49
  7.9 140.4 %all-gather.5.cloned.1.call-start = ((), (), s32[]{:S(2)}) async-start(), calls=%async_computation.2 | async-start | bytes 8650752 | tf_op jit(solution)/shard_map/all_gather | solution.py:53
  8.6 152.0 %copy-start.3 = (bf16[64,128]{1,0:T(8,128)(2,1)S(1)}, bf16[64,128]{1,0:T(8,128)(2,1)}, u32[]{:S(2)}) copy-start(bf16[64,128]{1,0:T(8,128)(2,1)} %param.9) | copy-start | bytes 49156
  8.7 152.0 %copy-start.2 = (bf16[512,1024]{1,0:T(8,128)(2,1)S(1)}, bf16[512,1024]{1,0:T(8,128)(2,1)}, u32[]{:S(2)}) copy-start(bf16[512,1024]{1,0:T(8,128)(2,1)} %param.7) | copy-start | bytes 3145732
  8.7 479.0 %reduce-scatter.2.cloned.1.call-start = ((), (), s32[]{:S(2)}) async-start(), calls=%async_computation.3 | async-start | bytes 17301504 | tf_op jit(solution)/shard_map/reduce_scatter | solution.py:79
  159.0 32.4 %collective-permute-start.1 = (bf16[127,1024]{1,0:T(8,128)(2,1)S(1)}, bf16[127,1024]{1,0:T(8,128)(2,1)}, u32[]{:S(2)}, u32[]{:S(2)}) collective-permute-start(bf16[127,1024]{1,0:T(8,128)(2,1)S(1)} %slice.44), channel_id=1, source_target_pairs={{8,0},{16,8},{24,16},{32,24},{40,32},{48,40},{56,48},{64,56},{72,6... | collective-permute-start | bytes 780296 | tf_op jit(solution)/shard_map/ppermute | solution.py:10
  200.0 1.2 copy-start.1
  203.4 9.4 %collective-permute-start = (bf16[127,1024]{0,1:T(8,128)(2,1)S(1)}, bf16[127,1024]{0,1:T(8,128)(2,1)}, u32[]{:S(2)}, u32[]{:S(2)}) collective-permute-start(bf16[127,1024]{0,1:T(8,128)(2,1)S(1)} %slice.38), channel_id=1, source_target_pairs={{0,8},{8,16},{16,24},{24,32},{32,40},{40,48},{48,56},{56,64},{64,7... | collective-permute-start | bytes 780296 | tf_op jit(solution)/shard_map/ppermute | solution.py:10
  217.3 4.5 copy-start
Sparse Core Ops, SparseCore 0:
  9.8 36.5 all-gather.2
  49.0 99.3 all-gather.4
  239.3 248.3 reduce-scatter.1
where the time goes:
time: 497 us; the launch traced here: 496 us
  waiting for transfers between devices  210 us (42%)
  blocking collectives  143 us (29%)
  local copies, waits for them, and re-layouts  72 us (14%)
  matrix products  35.4 us (7%)
  other arithmetic  15.1 us (3%)
  between operations  14 us (3%)
  starting transfers between devices  6.87 us (1%)
    psum x1, blocking collectives, on_device(): grad_filter = lax.psum(filter_part, 'ctx')  143 us
    all_gather x1, waiting for transfers between devices, on_device(): lax.all_gather(proj_out, 'ctx', axis=0, tiled=True)  102 us
    reduce_scatter x1, waiting for transfers between devices, on_device(): lax.psum_scatter(lax.dot_general(columns, gated, (((0,), (0,)), ((), ()))...  66 us
    all_gather x1, waiting for transfers between devices, on_device(): cot_full = lax.all_gather(cotangent, 'tp', axis=1, tiled=True)  37.7 us
    unnamed x17, local copies, waits for them, and re-layouts  20.2 us
    reshape x1, local copies, waits for them, and re-layouts, toeplitz_rows(): tiled.reshape(group_count, tap_count, 3 * tap_count - 1)  16.4 us
    reshape x1, local copies, waits for them, and re-layouts, on_device(): jnp.pad(corr.reshape(group_count, -1), ((0, 0), (0, tap_count)))  14.2 us
    dot_general x1, matrix products, on_device(): lax.dot_general(columns, gated, (((0,), (0,)), ((), ())), preferred_eleme...  12.8 us
  transfers between devices with their start and end apart: 5, of which 4 were waited for; matrix products, arithmetic and copies ran while one was open for 14% of the time, Pallas kernels for 0%

commit v1 on v0

--- a/solution.py
+++ b/solution.py
@@ -46,7 +46,9 @@
         "gts,bsgc->btgc", table, window, preferred_element_type=jnp.float32
     ).reshape(tok_rows, chan_width)
     gated = (query_in.astype(jnp.float32) * conv_out).astype(jnp.bfloat16)
-    cot_full = lax.all_gather(cotangent, "tp", axis=1, tiled=True)
+    cot_full = jnp.concatenate(
+        lax.all_to_all(jnp.stack([cotangent] * lax.axis_size("tp")), "tp", 0, 0), axis=1
+    )
     columns = cot_full
     grad_all = jnp.dot(
         columns,

time: 497 us -> 461 us (0.928)
  waiting for transfers between devices: 210 us -> 120 us
  blocking collectives: 143 us -> 196 us
    all_to_all x0 -> x1, blocking collectives: none -> 54.3 us  [on_device(): lax.all_to_all(jnp.stack([cotangent] * lax.axis_size('tp')), 'tp', 0, 0)]
    all_gather x1, waiting for transfers between devices: 102 us -> 47.9 us  [on_device(): lax.all_gather(proj_out, 'ctx', axis=0, tiled=True)]
    all_gather x1 -> x0, waiting for transfers between devices: 37.7 us -> none  [on_device(): cot_full = lax.all_gather(cotangent, 'tp', axis=1, tiled=True)]
    unnamed x17 -> x20, local copies, waits for them, and re-layouts: 20.2 us -> 22.8 us
  transfers between devices with their start and end apart: 5 -> 4, of which waited for: 4 -> 3; matrix products, arithmetic and copies ran while one was open for 14% -> 16% of each run, Pallas kernels for 0% -> 0%
where the time goes in v1:
time: 461 us; the launch traced here: 460 us
  blocking collectives  196 us (43%)
  waiting for transfers between devices  120 us (26%)
  local copies, waits for them, and re-layouts  75.9 us (16%)
  matrix products  33.8 us (7%)
  between operations  14.2 us (3%)
  other arithmetic  13.1 us (3%)
  starting transfers between devices  6.33 us (1%)
    psum x1, blocking collectives, on_device(): grad_filter = lax.psum(filter_part, 'ctx')  142 us
    reduce_scatter x1, waiting for transfers between devices, on_device(): lax.psum_scatter(lax.dot_general(columns, gated, (((0,), (0,)), ((), ()))...  68.4 us
    all_to_all x1, blocking collectives, on_device(): lax.all_to_all(jnp.stack([cotangent] * lax.axis_size('tp')), 'tp', 0, 0)  54.3 us
    all_gather x1, waiting for transfers between devices, on_device(): lax.all_gather(proj_out, 'ctx', axis=0, tiled=True)  47.9 us
    unnamed x20, local copies, waits for them, and re-layouts  22.8 us
    reshape x1, local copies, waits for them, and re-layouts, toeplitz_rows(): tiled.reshape(group_count, tap_count, 3 * tap_count - 1)  16.4 us
    reshape x1, local copies, waits for them, and re-layouts, on_device(): jnp.pad(corr.reshape(group_count, -1), ((0, 0), (0, tap_count)))  14.3 us
    dot_general x1, matrix products, on_device(): lax.dot_general(columns, gated, (((0,), (0,)), ((), ())), preferred_eleme...  13.5 us
  transfers between devices with their start and end apart: 4, of which 3 were waited for; matrix products, arithmetic and copies ran while one was open for 16% of the time, Pallas kernels for 0%

profile of v1, /device:TPU:8, one launch (start us, length us, event | category | flops | bytes accessed | tf_op | source)
XLA Modules:
  0.0 460.1 jit_solution(7392995141924976111)
XLA Ops:
  9.6 54.3 %all_to_all.5 = bf16[8,512,512]{1,2,0:T(8,128)(2,1)} all-to-all(bf16[8,512,512]{1,2,0:T(8,128)(2,1)S(1)} %stack.2), channel_id=1, replica_groups=mesh['ctx'=32,'tp'=8] {'tp'}, dimensions={0} | all-to-all | bytes 8388608 | tf_op jit(solution)/shard_map/all_to_all | solution.py:50
  63.9 47.9 %all-gather.2.cloned.1.call-done = bf16[4096,1024]{1,0:T(8,128)(2,1)} async-done(((bf16[128,1024]{1,0:T(8,128)(2,1)}), bf16[4096,1024]{1,0:T(8,128)(2,1)}) %all-gather.2.cloned.1.call-update) | async-done | bytes 8388624 | tf_op jit(solution)/shard_map/all_gather | solution.py:55
  111.8 10.7 %fusion.4 = (bf16[512,1024]{1,0:T(8,128)(2,1)S(1)}, f32[512,1024]{1,0:T(8,128)}) fusion(bf16[512,1024]{1,0:T(8,128)(2,1)} %param.6, bf16[512,4096]{0,1:T(8,128)(2,1)} %bitcast.71, bf16[4096,1024]{1,0:T(8,128)(2,1)} %all-gather.2.cloned.1.call-done), kind=kOutput, calls=%fused_computation.11 | convolution fusion | flops 4296540160 | bytes 16777216 | tf_op jit(solution)/shard_map/dot_general | solution.py:53
  124.8 2.3 copy.18
  127.7 4.1 copy.38
  131.8 3.1 slice.40
  134.8 16.4 %reshape.53 = bf16[64,128,383]{2,1,0:T(8,128)(2,1)} reshape(bf16[64,49024]{1,0:T(8,128)(2,1)} %slice.40) | data formatting | bytes 12550144 | tf_op jit(solution)/shard_map/reshape | solution.py:24
  159.0 2.3 fusion.6
  161.3 2.3 add_bitcast_fusion
  166.9 4.8 %collective-permute-start = (bf16[127,1024]{0,1:T(8,128)(2,1)S(1)}, bf16[127,1024]{0,1:T(8,128)(2,1)S(1)}, u32[]{:S(2)}, u32[]{:S(2)}) collective-permute-start(bf16[127,1024]{0,1:T(8,128)(2,1)S(1)} %slice.38), channel_id=1, source_target_pairs={{0,8},{8,16},{16,24},{24,32},{32,40},{40,48},{48,56},{56,64},{64,7... | collective-permute-start | bytes 780296 | tf_op jit(solution)/shard_map/ppermute | solution.py:10
  173.0 3.4 collective-permute-done
  179.8 3.7 fusion.8
  186.1 2.9 copy.23
  189.0 13.5 %convolution_bitcast_fusion = f32[4096,1024]{0,1:T(8,128)} fusion(bf16[512,4096]{0,1:T(8,128)(2,1)} %bitcast.72, f32[512,1024]{1,0:T(8,128)} %copy.23, bf16[512,1024]{1,0:T(8,128)(2,1)} %param.6), kind=kOutput, calls=%fused_computation | convolution fusion | flops 4296540160 | bytes 24117248 | tf_op jit(solution)/shard_map/dot_general | solution.py:82
  202.5 2.3 copy.32
  204.7 2.3 copy.31
  208.3 4.7 %copy.41 = f32[8,8,128,256]{3,1,2,0:T(8,128)S(1)} copy(f32[8,8,128,256]{3,2,1,0:T(8,128)S(1)} %bitcast.65) | data formatting | bytes 16777216
  213.0 3.9 pad.4
  216.9 14.3 %reshape.59 = f32[64,128,257]{2,1,0:T(8,128)} reshape(f32[64,32896]{1,0:T(8,128)} %pad.4) | data formatting | bytes 16842752 | tf_op jit(solution)/shard_map/reshape | solution.py:76
  231.3 6.4 %reduce_sum.9 = f32[64,257]{1,0:T(8,128)S(1)} reduce(f32[64,128,257]{2,1,0:T(8,128)} %reshape.59, f32[]{:T(128)} %constant.3.clone.1), dimensions={1}, to_apply=%region_0.1 | reduce | flops 2088896 | bytes 8487172 | tf_op jit(solution)/shard_map/reduce_sum | solution.py:79
  237.9 142.1 %psum.7 = f32[64,128]{1,0:T(8,128)} all-reduce(f32[64,128]{1,0:T(8,128)S(1)} %rev.9), channel_id=1, replica_groups=mesh['ctx'=32,'tp'=8] {'ctx'}, use_global_device_ids=true, to_apply=%region_1.2 | all-reduce | flops 8192 | bytes 65536 | tf_op jit(solution)/shard_map/psum | solution.py:89
  379.9 2.9 multiply_convert_fusion
  382.8 68.4 %reduce-scatter.2.cloned.1.call-done = f32[128,1024]{0,1:T(8,128)} async-done(((f32[4096,1024]{0,1:T(8,128)}), f32[128,1024]{0,1:T(8,128)}) %reduce-scatter.2.cloned.1.call-update) | async-done | bytes 524304 | tf_op jit(solution)/shard_map/reduce_scatter | solution.py:81
  451.2 2.0 copy.33
  (48 shorter events, 25.0 us)
Async XLA Ops:
  7.2 104.6 %all-gather.2.cloned.1.call-start = ((), (), s32[]{:S(2)}) async-start(), calls=%async_computation.2 | async-start | bytes 8650752 | tf_op jit(solution)/shard_map/all_gather | solution.py:55
  7.9 443.3 %reduce-scatter.2.cloned.1.call-start = ((), (), s32[]{:S(2)}) async-start(), calls=%async_computation.3 | async-start | bytes 17301504 | tf_op jit(solution)/shard_map/reduce_scatter | solution.py:81
  111.8 12.4 %copy-start.4 = (bf16[64,128]{1,0:T(8,128)(2,1)S(1)}, bf16[64,128]{1,0:T(8,128)(2,1)}, u32[]{:S(2)}) copy-start(bf16[64,128]{1,0:T(8,128)(2,1)} %param.9) | copy-start | bytes 49156
  111.8 12.4 %copy-start.3 = (bf16[512,1024]{1,0:T(8,128)(2,1)S(1)}, bf16[512,1024]{1,0:T(8,128)(2,1)}, u32[]{:S(2)}) copy-start(bf16[512,1024]{1,0:T(8,128)(2,1)} %param.7) | copy-start | bytes 3145732
  122.5 32.4 %collective-permute-start.1 = (bf16[127,1024]{1,0:T(8,128)(2,1)S(1)}, bf16[127,1024]{1,0:T(8,128)(2,1)}, u32[]{:S(2)}, u32[]{:S(2)}) collective-permute-start(bf16[127,1024]{1,0:T(8,128)(2,1)S(1)} %slice.44), channel_id=1, source_target_pairs={{8,0},{16,8},{24,16},{32,24},{40,32},{48,40},{56,48},{64,56},{72,6... | collective-permute-start | bytes 780296 | tf_op jit(solution)/shard_map/ppermute | solution.py:10
  163.6 1.2 copy-start.1
  166.9 9.4 %collective-permute-start = (bf16[127,1024]{0,1:T(8,128)(2,1)S(1)}, bf16[127,1024]{0,1:T(8,128)(2,1)S(1)}, u32[]{:S(2)}, u32[]{:S(2)}) collective-permute-start(bf16[127,1024]{0,1:T(8,128)(2,1)S(1)} %slice.38), channel_id=1, source_target_pairs={{0,8},{8,16},{16,24},{24,32},{32,40},{40,48},{48,56},{56,64},{64,7... | collective-permute-start | bytes 780296 | tf_op jit(solution)/shard_map/ppermute | solution.py:10
  177.8 1.6 copy-start.2
  231.3 148.6 %copy-start = (f32[512,1024]{1,0:T(8,128)S(1)}, f32[512,1024]{1,0:T(8,128)}, u32[]{:S(2)}) copy-start(f32[512,1024]{1,0:T(8,128)} %copy.23) | copy-start | bytes 6291460
Sparse Core Ops, SparseCore 0:
  10.6 101.1 all-gather.1
  202.6 248.5 reduce-scatter.1
